TPU v7x, 128 devices: a whole 4x4x4 slice. The times are simulated.
128 devices in a mesh: tm: 32 (over x, z, core), band: 4 (over y).
Axes of the slice: x: 4, y: 4, z: 4, core: 2. Of those that a mesh axis runs over, the one named last changes fastest.
Arguments:
- section_in: bfloat16 [64, 32, 8, 512], P('tm', 'band'), may hold values from -6 to 6
- norm_gain: float32 [512], replicated, may hold values from 0.1 to 1.9
- conv_weight: bfloat16 [3, 3, 3, 512, 512], replicated, may hold values from -0.0546875 to 0.0546875
- conv_bias: float32 [512], replicated, may hold values from -2 to 2
- lengths: int32 [4], replicated, may hold values from 1 to 48, as said below
- embed_weight: bfloat16 [512, 3072], replicated, may hold values from -0.25 to 0.25
- embed_bias: float32 [3072], replicated, may hold values from -3 to 3
- mod_shift: float32 [3072], replicated, may hold values from -3 to 3
- mod_scale: float32 [3072], replicated, may hold values from -1.5 to 1.5
- qkv_weight: bfloat16 [3072, 3, 12, 128], P(None, None, 'band'), may hold values from -0.109375 to 0.109375
- q_gain: float32 [128], replicated, may hold values from 1.2 to 6, as said below
- k_gain: float32 [128], replicated, may hold values from 1.2 to 6, as said below
Outputs:
- section_out: bfloat16 [64, 32, 8, 512], P('tm', 'band')
- attended: bfloat16 [16384, 12, 128], P('tm', 'band')
Inputs may be any that keep to these rules, and one draw needn't show every extreme that they name: `lengths`: whole frames of each clip; they sum to 64 and the longest clip has exactly 48 frames. `q_gain`: positive gains. `k_gain`: positive gains.
All inputs are finite; a program needn't handle non-finite values.
Results may differ from a plain program's by a relative error of at most 0.023.
The roundings to bfloat16 on the way count: a program that leaves them out, or rounds other values in their place, can miss the bound.
Values may be sent and summed in bfloat16 or wider, within the bound.
No kernel may reach another device: no remote copies, remote signals or barrier semaphores. Data moves between devices by JAX's collectives and lax.ppermute only.
A program may use at most 192 MiB of HBM per device.

v0:
```python
import jax
import jax.numpy as jnp
from jax import lax
from jax.sharding import PartitionSpec as P

EPSILON = 1e-06
KEY_BLOCK = 2048


def shifted(block, axis, distance):
    devices = range(lax.axis_size(axis))
    route = [(i - distance, i) for i in devices if i - distance in devices]
    return lax.ppermute(block, axis, route)


def extended(cells, sides, width):
    for axis, dim in sides:
        count = lax.axis_size(axis)
        ends = count - 1
        head = lax.slice_in_dim(cells, 0, width, axis=dim)
        tail = lax.slice_in_dim(cells, cells.shape[dim] - width, cells.shape[dim], axis=dim)
        cells = jnp.concatenate(
            [
                lax.ppermute(tail, axis, [(i, (i + 1) % count) for i in range(ends)]),
                cells,
                lax.ppermute(head, axis, [((i + 1) % count, i) for i in range(ends)]),
            ],
            axis=dim,
        )
    return cells


def clip_layout(frame_index, lengths):
    clip_ends = jnp.cumsum(lengths)
    starts = clip_ends - lengths
    member = (frame_index[:, None] >= clip_ends[None, :]).astype(jnp.int32)
    clip_id = jnp.sum(member, axis=1)
    labels = jnp.arange(lengths.shape[0], dtype=jnp.int32)
    clip_first = jnp.sum(jnp.where(clip_id[:, None] == labels[None, :], starts[None, :], 0), axis=1)
    return (clip_id, clip_first)


def rms_scale(values, gain):
    mean_square = jnp.mean(values * values, axis=-1, keepdims=True)
    return values * lax.rsqrt(mean_square + EPSILON) * gain


def modulate(token_block, embed_weight, embed_bias, mod_shift, mod_scale):
    embedded = jnp.dot(token_block, embed_weight, preferred_element_type=jnp.float32) + embed_bias
    center = embedded - jnp.mean(embedded, axis=-1, keepdims=True)
    spread = jnp.mean(center * center, axis=-1, keepdims=True)
    normal = center * lax.rsqrt(spread + EPSILON)
    return (normal * (1.0 + mod_scale) + mod_shift).astype(jnp.bfloat16)


def over_blocks(block_fn, carry, pieces):
    rows = pieces[0].shape[0]
    count = rows // KEY_BLOCK
    stacked = tuple((piece.reshape((count, KEY_BLOCK) + piece.shape[1:]) for piece in pieces))
    offsets = KEY_BLOCK * jnp.arange(count, dtype=jnp.int32)

    def step(current, item):
        return (block_fn(current, item[0], item[1]), None)

    carry, unused = lax.scan(step, carry, (stacked, offsets))
    return carry


def per_device(
    section_in,
    norm_gain,
    conv_weight,
    conv_bias,
    lengths,
    embed_weight,
    embed_bias,
    mod_shift,
    mod_scale,
    qkv_weight,
    q_gain,
    k_gain,
):
    frames_dev, rows_dev, frame_width, channels = section_in.shape
    tm_place = lax.axis_index("tm")
    own_frames = tm_place * frames_dev + jnp.arange(frames_dev, dtype=jnp.int32)
    own_clip, own_first = clip_layout(own_frames, lengths)
    inputs = section_in.astype(jnp.float32)
    active = jax.nn.silu(rms_scale(inputs, norm_gain)).astype(jnp.bfloat16)
    earlier = shifted(active, "tm", 1)
    widened = jnp.concatenate([earlier, active], axis=0)
    widened = extended(widened, (("band", 1),), 1)
    widened = jnp.pad(widened, ((0, 0), (0, 0), (1, 1), (0, 0)))
    columns = jnp.concatenate(
        [widened[:, :, shift_col : shift_col + frame_width] for shift_col in range(3)], axis=-1
    )
    slot_ids = jnp.arange(frames_dev + 2, dtype=jnp.int32)
    conv_sum = jnp.zeros((frames_dev * rows_dev * frame_width, channels), jnp.float32)
    for tap_time in range(3):
        source = jnp.maximum(own_frames - 2 + tap_time, own_first) - (tm_place * frames_dev - 2)
        chooser = (source[:, None] == slot_ids[None, :]).astype(jnp.bfloat16)
        tapped = jnp.einsum(
            "ij,jhwc->ihwc", chooser, columns, preferred_element_type=jnp.float32
        ).astype(jnp.bfloat16)
        for tap_row in range(3):
            tap_piece = tapped[:, tap_row : tap_row + rows_dev].reshape(-1, 3 * channels)
            tap_weight = conv_weight[tap_time, tap_row].reshape(3 * channels, channels)
            conv_sum = conv_sum + jnp.dot(tap_piece, tap_weight, preferred_element_type=jnp.float32)
    section_out = (
        inputs + conv_bias + conv_sum.reshape(frames_dev, rows_dev, frame_width, channels)
    ).astype(jnp.bfloat16)
    piece = lax.all_gather(section_out, "band", axis=1, tiled=True)
    local_rows = modulate(
        piece.reshape(-1, channels), embed_weight, embed_bias, mod_shift, mod_scale
    )
    modulated = local_rows.reshape(frames_dev, piece.shape[1], frame_width, -1)
    model_width = embed_weight.shape[1]
    modulated = modulated.reshape(-1, model_width)
    token_count = modulated.shape[0]
    frame_tok = token_count // frames_dev
    heads_here = qkv_weight.shape[2]
    head_size = qkv_weight.shape[3]
    projected = jnp.dot(
        modulated, qkv_weight.reshape(model_width, -1), preferred_element_type=jnp.float32
    )
    projected = projected.reshape(token_count, 3, heads_here, head_size)
    queries = rms_scale(projected[:, 0], q_gain).astype(jnp.bfloat16)
    key_rows = rms_scale(projected[:, 1], k_gain).astype(jnp.bfloat16)
    values = projected[:, 2].astype(jnp.bfloat16)
    query_clip = jnp.repeat(own_clip, frame_tok)
    score_scale = 1.0 / head_size**0.5

    def masked_scores(key_piece, start):
        key_tokens = start + jnp.arange(key_piece.shape[0], dtype=jnp.int32)
        key_clip, unused_first = clip_layout(key_tokens // frame_tok, lengths)
        same_clip = (query_clip[:, None] == key_clip[None, :])[None, :, :]
        scores = (
            jnp.einsum("qhd,khd->hqk", queries, key_piece, preferred_element_type=jnp.float32)
            * score_scale
        )
        return (jnp.where(same_clip, scores, -1e30), same_clip)

    def running_block(carry, pieces, start):
        old_peak, total, mixed = carry
        masked, same_clip = masked_scores(pieces[0], start)
        new_peak = jnp.maximum(old_peak, jnp.max(masked, axis=-1))
        factor = jnp.exp(old_peak - new_peak)
        weights = jnp.where(same_clip, jnp.exp(masked - new_peak[:, :, None]), 0.0)
        total = total * factor + jnp.sum(weights, axis=-1)
        mixed = mixed * jnp.transpose(factor)[:, :, None] + jnp.einsum(
            "hqk,khd->qhd",
            weights.astype(jnp.bfloat16),
            pieces[1],
            preferred_element_type=jnp.float32,
        )
        return (new_peak, total, mixed)

    peak_start = jnp.full((heads_here, token_count), -1e30, jnp.float32)
    total_start = jnp.zeros((heads_here, token_count), jnp.float32)
    mixed_start = jnp.zeros((token_count, heads_here, head_size), jnp.float32)
    unused_peak, weight_sum, mixed_rows = over_blocks(
        running_block,
        (peak_start, total_start, mixed_start),
        (
            lax.all_gather(key_rows, "tm", axis=0, tiled=True),
            lax.all_gather(values, "tm", axis=0, tiled=True),
        ),
    )
    attended = (mixed_rows / jnp.transpose(weight_sum)[:, :, None]).astype(jnp.bfloat16)
    return (section_out, attended)


def solution(mesh):
    return jax.shard_map(
        per_device,
        mesh=mesh,
        in_specs=(
            P("tm", "band", None, None),
            P(),
            P(),
            P(),
            P(),
            P(),
            P(),
            P(),
            P(),
            P(None, None, "band", None),
            P(),
            P(),
        ),
        out_specs=(P("tm", "band", None, None), P("tm", "band", None)),
        check_vma=False,
    )
```

profile of v0, /device:TPU:2, one launch (start us, length us, event | category | flops | bytes accessed | tf_op | source)
XLA Modules:
  0.0 441.7 jit_solution(10665938197625043232)
XLA Ops:
  12.9 9.5 %fusion.73 = (bf16[1,1,3,512,512]{4,3,2,1,0:T(8,128)(2,1)}, bf16[1,1,3,512,512]{4,3,2,1,0:T(8,128)(2,1)}, bf16[1,1,3,512,512]{4,3,2,1,0:T(8,128)(2,1)}, bf16[1,1...) fusion(bf16[3,3,3,512,512]{4,3,2,1,0:T(8,128)(2,1)} %param.16), kind=kLoop, calls=%fused_computation.123 | loop fusion | bytes 28311552 | tf_op jit(solution)/shard_map/slice | solution.py:106
  23.2 3.5 collective-permute-start.1
  28.5 10.3 %copy.95 = bf16[3072,3,3,128]{0,3,2,1:T(8,128)(2,1)} copy(bf16[3072,3,3,128]{3,0,2,1:T(8,128)(2,1)} %param.23) | data formatting | bytes 14155776 | tf_op args[9]
  51.0 15.2 %all_gather.9 = bf16[2,32,8,512]{3,2,0,1:T(8,128)(2,1)S(1)} all-gather(bf16[2,8,8,512]{3,2,0,1:T(8,128)(2,1)S(1)} %copy.93), channel_id=1, replica_groups=mesh['tm'=32,'band'=4] {'band'}, dimensions={1}, use_global_device_ids=true | all-gather | bytes 655360 | tf_op jit(solution)/shard_map/all_gather | solution.py:111
  69.3 4.3 fusion.33
  76.3 70.3 %all-gather.4.cloned.1.call-done = bf16[16384,3,128]{0,2,1:T(8,128)(2,1)} async-done(((bf16[512,3,128]{0,2,1:T(8,128)(2,1)}), bf16[16384,3,128]{0,2,1:T(8,128)(2,1)}) %all-gather.4.cloned.1.call-update) | async-done | bytes 12582928 | tf_op jit(solution)/shard_map/all_gather | solution.py:164
  146.6 14.6 %copy.106 = bf16[48,8,8,2048]{3,2,1,0:T(8,128)(2,1)} copy(bf16[48,8,8,2048]{3,1,2,0:T(8,128)(2,1)} %bitcast.162) | data formatting | bytes 25165824
  161.2 17.1 %copy.96 = bf16[8,2048,3,128]{3,1,2,0:T(8,128)(2,1)} copy(bf16[8,2048,3,128]{1,0,3,2:T(8,128)(2,1)} %bitcast.160) | data formatting | bytes 25165824
  178.3 40.6 %all-gather.6.cloned.1.call-done = bf16[16384,1,3,128]{0,3,2,1:T(8,128)(2,1)} async-done(((bf16[512,1,3,128]{0,3,2,1:T(8,128)(2,1)}), bf16[16384,1,3,128]{0,3,2,1:T(8,128)(2,1)}) %all-gather.6.cloned.1.call-update) | async-done | bytes 12582928 | tf_op jit(solution)/shard_map/all_gather | solution.py:165
  218.9 11.7 %copy.107 = bf16[48,8,8,2048]{3,2,1,0:T(8,128)(2,1)S(1)} copy(bf16[48,8,8,2048]{3,1,2,0:T(8,128)(2,1)} %bitcast.163) | data formatting | bytes 25165824
  230.6 16.5 %copy.98 = bf16[8,2048,3,128]{1,3,2,0:T(8,128)(2,1)} copy(bf16[8,2048,3,128]{1,0,3,2:T(8,128)(2,1)S(1)} %bitcast.161) | data formatting | bytes 25165824
  247.1 183.2 %while.17 = (s32[]{:T(128)}, f32[3,512]{1,0:T(4,128)S(1)}, f32[3,512]{1,0:T(4,128)S(1)}, f32[512,3,128]{0,2,1:T(8,128)}, s32[8]{0:T(128)S(1)}, /*index=5*/s32[1,...) while((s32[]{:T(128)}, f32[3,512]{1,0:T(4,128)S(1)}, ...), condition=%wide.region_13.14_spmd.clone, body=%wide.region_9.13_spmd.clone.sunk | while | flops 1653210112 | bytes 97526976 | solution.py:65
  249.3 7.4 %fusion.111 = (f32[3,512]{1,0:T(4,128)S(1)}, f32[3,2048,512]{2,1,0:T(8,128)}) fusion(pred[512,2048]{0,1:T(8,128)(4,1)S(1)} %broadcast_compare_fusion.2, bf16[512,3,128]{2,0,1:T(8,128)(2,1)S(1)} %get-tuple-element.384, bf16[8,2048,3,128]{3,1,2,0:T(8,128)(2,1)} %get-tuple-element.383, s32[]{:T(128)} %get-tuple-element.365), kind=kOutput, calls=%fused_computation.3.clone.1 | convolution fusion | flops 814742016 | bytes 15604224 | tf_op jit(solution)/shard_map/while/body/eval_jaxpr/qhd,khd->hqk/dot_general | solution.py:137
  256.7 9.9 %fusion.115 = f32[512,3,128]{0,2,1:T(8,128)} fusion(f32[3,2048,512]{2,1,0:T(8,128)} %get-tuple-element.351, f32[3,512]{1,0:T(4,128)S(1)} %get-tuple-element.378, pred[512,2048]{0,1:T(8,128)(4,1)S(1)} %broadcast_compare_fusion.2, bf16[8,2048,3,128]{1,3,2,0:T(8,128)(2,1)} %get-tuple-element.385, s32[]{:T(128)} %get-tuple-element.365, ...), kind=kOutput, calls=%fused_computation.15.clone.1 | convolution fusion | flops 821624832 | bytes 16790016 | tf_op jit(solution)/shard_map/while/body/eval_jaxpr/hqk,khd->qhd/dot_general | solution.py:149
  266.6 3.3 fusion.113
  272.1 7.4 %fusion.111 = (f32[3,512]{1,0:T(4,128)S(1)}, f32[3,2048,512]{2,1,0:T(8,128)}) fusion(pred[512,2048]{0,1:T(8,128)(4,1)S(1)} %broadcast_compare_fusion.2, bf16[512,3,128]{2,0,1:T(8,128)(2,1)S(1)} %get-tuple-element.384, bf16[8,2048,3,128]{3,1,2,0:T(8,128)(2,1)} %get-tuple-element.383, s32[]{:T(128)} %get-tuple-element.365), kind=kOutput, calls=%fused_computation.3.clone.1 | convolution fusion | flops 814742016 | bytes 15604224 | tf_op jit(solution)/shard_map/while/body/eval_jaxpr/qhd,khd->hqk/dot_general | solution.py:137
  279.5 10.0 %fusion.115 = f32[512,3,128]{0,2,1:T(8,128)} fusion(f32[3,2048,512]{2,1,0:T(8,128)} %get-tuple-element.351, f32[3,512]{1,0:T(4,128)S(1)} %get-tuple-element.378, pred[512,2048]{0,1:T(8,128)(4,1)S(1)} %broadcast_compare_fusion.2, bf16[8,2048,3,128]{1,3,2,0:T(8,128)(2,1)} %get-tuple-element.385, s32[]{:T(128)} %get-tuple-element.365, ...), kind=kOutput, calls=%fused_computation.15.clone.1 | convolution fusion | flops 821624832 | bytes 16790016 | tf_op jit(solution)/shard_map/while/body/eval_jaxpr/hqk,khd->qhd/dot_general | solution.py:149
  289.5 3.3 fusion.113
  295.0 7.4 %fusion.111 = (f32[3,512]{1,0:T(4,128)S(1)}, f32[3,2048,512]{2,1,0:T(8,128)}) fusion(pred[512,2048]{0,1:T(8,128)(4,1)S(1)} %broadcast_compare_fusion.2, bf16[512,3,128]{2,0,1:T(8,128)(2,1)S(1)} %get-tuple-element.384, bf16[8,2048,3,128]{3,1,2,0:T(8,128)(2,1)} %get-tuple-element.383, s32[]{:T(128)} %get-tuple-element.365), kind=kOutput, calls=%fused_computation.3.clone.1 | convolution fusion | flops 814742016 | bytes 15604224 | tf_op jit(solution)/shard_map/while/body/eval_jaxpr/qhd,khd->hqk/dot_general | solution.py:137
  302.4 10.0 %fusion.115 = f32[512,3,128]{0,2,1:T(8,128)} fusion(f32[3,2048,512]{2,1,0:T(8,128)} %get-tuple-element.351, f32[3,512]{1,0:T(4,128)S(1)} %get-tuple-element.378, pred[512,2048]{0,1:T(8,128)(4,1)S(1)} %broadcast_compare_fusion.2, bf16[8,2048,3,128]{1,3,2,0:T(8,128)(2,1)} %get-tuple-element.385, s32[]{:T(128)} %get-tuple-element.365, ...), kind=kOutput, calls=%fused_computation.15.clone.1 | convolution fusion | flops 821624832 | bytes 16790016 | tf_op jit(solution)/shard_map/while/body/eval_jaxpr/hqk,khd->qhd/dot_general | solution.py:149
  312.4 3.3 fusion.113
  317.9 7.4 %fusion.111 = (f32[3,512]{1,0:T(4,128)S(1)}, f32[3,2048,512]{2,1,0:T(8,128)}) fusion(pred[512,2048]{0,1:T(8,128)(4,1)S(1)} %broadcast_compare_fusion.2, bf16[512,3,128]{2,0,1:T(8,128)(2,1)S(1)} %get-tuple-element.384, bf16[8,2048,3,128]{3,1,2,0:T(8,128)(2,1)} %get-tuple-element.383, s32[]{:T(128)} %get-tuple-element.365), kind=kOutput, calls=%fused_computation.3.clone.1 | convolution fusion | flops 814742016 | bytes 15604224 | tf_op jit(solution)/shard_map/while/body/eval_jaxpr/qhd,khd->hqk/dot_general | solution.py:137
  325.3 10.0 %fusion.115 = f32[512,3,128]{0,2,1:T(8,128)} fusion(f32[3,2048,512]{2,1,0:T(8,128)} %get-tuple-element.351, f32[3,512]{1,0:T(4,128)S(1)} %get-tuple-element.378, pred[512,2048]{0,1:T(8,128)(4,1)S(1)} %broadcast_compare_fusion.2, bf16[8,2048,3,128]{1,3,2,0:T(8,128)(2,1)} %get-tuple-element.385, s32[]{:T(128)} %get-tuple-element.365, ...), kind=kOutput, calls=%fused_computation.15.clone.1 | convolution fusion | flops 821624832 | bytes 16790016 | tf_op jit(solution)/shard_map/while/body/eval_jaxpr/hqk,khd->qhd/dot_general | solution.py:149
  335.3 3.3 fusion.113
  340.8 7.4 %fusion.111 = (f32[3,512]{1,0:T(4,128)S(1)}, f32[3,2048,512]{2,1,0:T(8,128)}) fusion(pred[512,2048]{0,1:T(8,128)(4,1)S(1)} %broadcast_compare_fusion.2, bf16[512,3,128]{2,0,1:T(8,128)(2,1)S(1)} %get-tuple-element.384, bf16[8,2048,3,128]{3,1,2,0:T(8,128)(2,1)} %get-tuple-element.383, s32[]{:T(128)} %get-tuple-element.365), kind=kOutput, calls=%fused_computation.3.clone.1 | convolution fusion | flops 814742016 | bytes 15604224 | tf_op jit(solution)/shard_map/while/body/eval_jaxpr/qhd,khd->hqk/dot_general | solution.py:137
  348.2 10.0 %fusion.115 = f32[512,3,128]{0,2,1:T(8,128)} fusion(f32[3,2048,512]{2,1,0:T(8,128)} %get-tuple-element.351, f32[3,512]{1,0:T(4,128)S(1)} %get-tuple-element.378, pred[512,2048]{0,1:T(8,128)(4,1)S(1)} %broadcast_compare_fusion.2, bf16[8,2048,3,128]{1,3,2,0:T(8,128)(2,1)} %get-tuple-element.385, s32[]{:T(128)} %get-tuple-element.365, ...), kind=kOutput, calls=%fused_computation.15.clone.1 | convolution fusion | flops 821624832 | bytes 16790016 | tf_op jit(solution)/shard_map/while/body/eval_jaxpr/hqk,khd->qhd/dot_general | solution.py:149
  363.7 7.4 %fusion.111 = (f32[3,512]{1,0:T(4,128)S(1)}, f32[3,2048,512]{2,1,0:T(8,128)}) fusion(pred[512,2048]{0,1:T(8,128)(4,1)S(1)} %broadcast_compare_fusion.2, bf16[512,3,128]{2,0,1:T(8,128)(2,1)S(1)} %get-tuple-element.384, bf16[8,2048,3,128]{3,1,2,0:T(8,128)(2,1)} %get-tuple-element.383, s32[]{:T(128)} %get-tuple-element.365), kind=kOutput, calls=%fused_computation.3.clone.1 | convolution fusion | flops 814742016 | bytes 15604224 | tf_op jit(solution)/shard_map/while/body/eval_jaxpr/qhd,khd->hqk/dot_general | solution.py:137
  371.1 10.0 %fusion.115 = f32[512,3,128]{0,2,1:T(8,128)} fusion(f32[3,2048,512]{2,1,0:T(8,128)} %get-tuple-element.351, f32[3,512]{1,0:T(4,128)S(1)} %get-tuple-element.378, pred[512,2048]{0,1:T(8,128)(4,1)S(1)} %broadcast_compare_fusion.2, bf16[8,2048,3,128]{1,3,2,0:T(8,128)(2,1)} %get-tuple-element.385, s32[]{:T(128)} %get-tuple-element.365, ...), kind=kOutput, calls=%fused_computation.15.clone.1 | convolution fusion | flops 821624832 | bytes 16790016 | tf_op jit(solution)/shard_map/while/body/eval_jaxpr/hqk,khd->qhd/dot_general | solution.py:149
  386.6 7.4 %fusion.111 = (f32[3,512]{1,0:T(4,128)S(1)}, f32[3,2048,512]{2,1,0:T(8,128)}) fusion(pred[512,2048]{0,1:T(8,128)(4,1)S(1)} %broadcast_compare_fusion.2, bf16[512,3,128]{2,0,1:T(8,128)(2,1)S(1)} %get-tuple-element.384, bf16[8,2048,3,128]{3,1,2,0:T(8,128)(2,1)} %get-tuple-element.383, s32[]{:T(128)} %get-tuple-element.365), kind=kOutput, calls=%fused_computation.3.clone.1 | convolution fusion | flops 814742016 | bytes 15604224 | tf_op jit(solution)/shard_map/while/body/eval_jaxpr/qhd,khd->hqk/dot_general | solution.py:137
  394.1 10.0 %fusion.115 = f32[512,3,128]{0,2,1:T(8,128)} fusion(f32[3,2048,512]{2,1,0:T(8,128)} %get-tuple-element.351, f32[3,512]{1,0:T(4,128)S(1)} %get-tuple-element.378, pred[512,2048]{0,1:T(8,128)(4,1)S(1)} %broadcast_compare_fusion.2, bf16[8,2048,3,128]{1,3,2,0:T(8,128)(2,1)} %get-tuple-element.385, s32[]{:T(128)} %get-tuple-element.365, ...), kind=kOutput, calls=%fused_computation.15.clone.1 | convolution fusion | flops 821624832 | bytes 16790016 | tf_op jit(solution)/shard_map/while/body/eval_jaxpr/hqk,khd->qhd/dot_general | solution.py:149
  409.6 7.4 %fusion.111 = (f32[3,512]{1,0:T(4,128)S(1)}, f32[3,2048,512]{2,1,0:T(8,128)}) fusion(pred[512,2048]{0,1:T(8,128)(4,1)S(1)} %broadcast_compare_fusion.2, bf16[512,3,128]{2,0,1:T(8,128)(2,1)S(1)} %get-tuple-element.384, bf16[8,2048,3,128]{3,1,2,0:T(8,128)(2,1)} %get-tuple-element.383, s32[]{:T(128)} %get-tuple-element.365), kind=kOutput, calls=%fused_computation.3.clone.1 | convolution fusion | flops 814742016 | bytes 15604224 | tf_op jit(solution)/shard_map/while/body/eval_jaxpr/qhd,khd->hqk/dot_general | solution.py:137
  417.0 10.0 %fusion.115 = f32[512,3,128]{0,2,1:T(8,128)} fusion(f32[3,2048,512]{2,1,0:T(8,128)} %get-tuple-element.351, f32[3,512]{1,0:T(4,128)S(1)} %get-tuple-element.378, pred[512,2048]{0,1:T(8,128)(4,1)S(1)} %broadcast_compare_fusion.2, bf16[8,2048,3,128]{1,3,2,0:T(8,128)(2,1)} %get-tuple-element.385, s32[]{:T(128)} %get-tuple-element.365, ...), kind=kOutput, calls=%fused_computation.15.clone.1 | convolution fusion | flops 821624832 | bytes 16790016 | tf_op jit(solution)/shard_map/while/body/eval_jaxpr/hqk,khd->qhd/dot_general | solution.py:149
  (211 shorter events, 61.0 us)
Async XLA Ops:
  7.2 59.1 %copy-start = (bf16[512,3072]{1,0:T(8,128)(2,1)S(1)}, bf16[512,3072]{1,0:T(8,128)(2,1)}, u32[]{:S(2)}) copy-start(bf16[512,3072]{1,0:T(8,128)(2,1)} %param.19) | copy-start | bytes 9437188
  7.2 139.4 %all-gather.4.cloned.1.call-start = ((), (), s32[]{:S(2)}) async-start(), calls=%async_computation | async-start | bytes 12976128 | tf_op jit(solution)/shard_map/all_gather | solution.py:164
  9.5 13.4 %collective-permute-start = (bf16[2,8,8,512]{3,2,1,0:T(8,128)(2,1)S(1)}, bf16[2,8,8,512]{3,2,1,0:T(8,128)(2,1)S(1)}, u32[]{:S(2)}, u32[]{:S(2)}) collective-permute-start(bf16[2,8,8,512]{3,2,1,0:T(8,128)(2,1)S(1)} %fusion.58), channel_id=1, source_target_pairs={{0,4},{4,8},{8,12},{12,16},{16,20},{20,24},{24,28},{28,32},{32,36}... | collective-permute-start | bytes 393224 | tf_op jit(solution)/shard_map/ppermute | solution.py:13
  12.9 9.6 %copy-start.17 = (f32[3072]{0:T(1024)S(1)}, f32[3072]{0:T(1024)}, u32[]{:S(2)}) copy-start(f32[3072]{0:T(1024)} %param.22) | copy-start | bytes 36868
  23.2 15.6 %collective-permute-start.1 = (bf16[4,1,8,512]{3,2,1,0:T(8,128)(2,1)S(1)}, bf16[4,1,8,512]{3,2,1,0:T(8,128)(2,1)S(1)}, u32[]{:S(2)}, u32[]{:S(2)}) collective-permute-start(bf16[4,1,8,512]{3,2,1,0:T(8,128)(2,1)S(1)} %get-tuple-element.275), channel_id=1, source_target_pairs={{0,1},{1,2},{2,3},{4,5},{5,6},{6,7},{8,9},{9,10},{10,11},{12,13},{... | collective-permute-start | bytes 98312 | tf_op jit(solution)/shard_map/ppermute | solution.py:24
  26.6 12.1 %collective-permute-start.2 = (bf16[4,1,8,512]{3,2,1,0:T(8,128)(2,1)S(1)}, bf16[4,1,8,512]{3,2,1,0:T(8,128)(2,1)S(1)}, u32[]{:S(2)}, u32[]{:S(2)}) collective-permute-start(bf16[4,1,8,512]{3,2,1,0:T(8,128)(2,1)S(1)} %get-tuple-element.276), channel_id=1, source_target_pairs={{1,0},{2,1},{3,2},{5,4},{6,5},{7,6},{9,8},{10,9},{11,10},{13,12},{... | collective-permute-start | bytes 98312 | tf_op jit(solution)/shard_map/ppermute | solution.py:26
  39.4 2.1 copy-start.21
  43.7 2.2 copy-start.11
  44.6 1.6 copy-start.10
  45.8 1.8 copy-start.8
  46.2 1.9 copy-start.7
  47.2 1.6 copy-start.6
  47.7 1.6 copy-start.5
  48.9 1.6 copy-start.3
  49.8 16.5 %copy-start.16 = (f32[3072]{0:T(1024)S(1)}, f32[3072]{0:T(1024)}, u32[]{:S(2)}) copy-start(f32[3072]{0:T(1024)} %param.20) | copy-start | bytes 36868
  50.9 17.2 %copy-start.13 = (bf16[2,8,8,512]{3,2,1,0:T(8,128)(2,1)}, bf16[2,8,8,512]{3,2,1,0:T(8,128)(2,1)S(1)}, u32[]{:S(2)}) copy-start(bf16[2,8,8,512]{3,2,1,0:T(8,128)(2,1)S(1)} %fusion.50) | copy-start | bytes 393220
  66.2 3.0 slice-start
  66.3 3.0 slice-start.1
  69.3 4.5 %copy-start.19 = (f32[128]{0:T(128)S(1)}, f32[128]{0:T(128)}, u32[]{:S(2)}) copy-start(f32[128]{0:T(128)} %param.24) | copy-start | bytes 1540
  69.3 4.5 %copy-start.20 = (f32[128]{0:T(128)S(1)}, f32[128]{0:T(128)}, u32[]{:S(2)}) copy-start(f32[128]{0:T(128)} %param.25) | copy-start | bytes 1540
  73.6 2.3 copy-start.24
  74.8 144.1 %all-gather.6.cloned.1.call-start = ((), (), s32[]{:S(2)}) async-start(), calls=%async_computation.1 | async-start | bytes 12976128 | tf_op jit(solution)/shard_map/all_gather | solution.py:165
  230.6 16.5 %copy-start.15 = (s32[2]{0:T(128)S(1)}, s32[2]{0:T(128)}, u32[]{:S(2)}) copy-start(s32[2]{0:T(128)} %copy-done.14) | copy-start | bytes 28
  256.7 9.9 %copy-start.2 = (f32[3,2048,512]{2,1,0:T(8,128)S(1)}, f32[3,2048,512]{2,1,0:T(8,128)}, u32[]{:S(2)}) copy-start(f32[3,2048,512]{2,1,0:T(8,128)} %get-tuple-element.351) | copy-start | bytes 37748740 | tf_op jit(solution)/shard_map/while
  279.5 10.0 %copy-start.2 = (f32[3,2048,512]{2,1,0:T(8,128)S(1)}, f32[3,2048,512]{2,1,0:T(8,128)}, u32[]{:S(2)}) copy-start(f32[3,2048,512]{2,1,0:T(8,128)} %get-tuple-element.351) | copy-start | bytes 37748740 | tf_op jit(solution)/shard_map/while
  302.4 10.0 %copy-start.2 = (f32[3,2048,512]{2,1,0:T(8,128)S(1)}, f32[3,2048,512]{2,1,0:T(8,128)}, u32[]{:S(2)}) copy-start(f32[3,2048,512]{2,1,0:T(8,128)} %get-tuple-element.351) | copy-start | bytes 37748740 | tf_op jit(solution)/shard_map/while
  325.3 10.0 %copy-start.2 = (f32[3,2048,512]{2,1,0:T(8,128)S(1)}, f32[3,2048,512]{2,1,0:T(8,128)}, u32[]{:S(2)}) copy-start(f32[3,2048,512]{2,1,0:T(8,128)} %get-tuple-element.351) | copy-start | bytes 37748740 | tf_op jit(solution)/shard_map/while
  348.2 10.0 %copy-start.2 = (f32[3,2048,512]{2,1,0:T(8,128)S(1)}, f32[3,2048,512]{2,1,0:T(8,128)}, u32[]{:S(2)}) copy-start(f32[3,2048,512]{2,1,0:T(8,128)} %get-tuple-element.351) | copy-start | bytes 37748740 | tf_op jit(solution)/shard_map/while
  371.1 10.0 %copy-start.2 = (f32[3,2048,512]{2,1,0:T(8,128)S(1)}, f32[3,2048,512]{2,1,0:T(8,128)}, u32[]{:S(2)}) copy-start(f32[3,2048,512]{2,1,0:T(8,128)} %get-tuple-element.351) | copy-start | bytes 37748740 | tf_op jit(solution)/shard_map/while
  394.0 10.0 %copy-start.2 = (f32[3,2048,512]{2,1,0:T(8,128)S(1)}, f32[3,2048,512]{2,1,0:T(8,128)}, u32[]{:S(2)}) copy-start(f32[3,2048,512]{2,1,0:T(8,128)} %get-tuple-element.351) | copy-start | bytes 37748740 | tf_op jit(solution)/shard_map/while
  417.0 10.0 %copy-start.2 = (f32[3,2048,512]{2,1,0:T(8,128)S(1)}, f32[3,2048,512]{2,1,0:T(8,128)}, u32[]{:S(2)}) copy-start(f32[3,2048,512]{2,1,0:T(8,128)} %get-tuple-element.351) | copy-start | bytes 37748740 | tf_op jit(solution)/shard_map/while
  430.3 4.6 %copy-start.1 = (bf16[512,3072]{1,0:T(8,128)(2,1)S(1)}, bf16[512,3072]{1,0:T(8,128)(2,1)}, u32[]{:S(2)}) copy-start(bf16[512,3072]{1,0:T(8,128)(2,1)} %param.19) | copy-start | bytes 9437188
  (7 other events, 8.6 us)
Sparse Core Ops, SparseCore 0:
  74.9 71.6 all-gather.3
  148.8 70.0 all-gather.5
where the time goes:
time: 445 us; the launch traced here: 442 us
  matrix products  151 us (34%)
  waiting for transfers between devices  111 us (25%)
  local copies, waits for them, and re-layouts  94.5 us (21%)
  other arithmetic  47.8 us (11%)
  blocking collectives  15.2 us (3%)
  between operations  14.6 us (3%)
  starting transfers between devices  6.98 us (2%)
    dot_general x8, matrix products, running_block(): jnp.einsum('hqk,khd->qhd', weights.astype(jnp.bfloat16), pieces[1], prefe...  79.8 us
    unnamed x58, local copies, waits for them, and re-layouts  72.6 us
    all_gather x1, waiting for transfers between devices, per_device(): lax.all_gather(key_rows, 'tm', axis=0, tiled=True)  70.3 us
    dot_general x8, matrix products, masked_scores(): jnp.einsum('qhd,khd->hqk', queries, key_piece, preferred_element_type=jnp...  59.1 us
    all_gather x1, waiting for transfers between devices, per_device(): lax.all_gather(values, 'tm', axis=0, tiled=True)  40.6 us
    reduce_sum x8, other arithmetic, running_block(): total = total * factor + jnp.sum(weights, axis=-1)  26.2 us
    all_gather x1, blocking collectives, per_device(): piece = lax.all_gather(section_out, 'band', axis=1, tiled=True)  15.2 us
    slice x1, local copies, waits for them, and re-layouts, per_device(): tap_weight = conv_weight[tap_time, tap_row].reshape(3 * channels, channels)  9.55 us
  transfers between devices with their start and end apart: 5, of which 2 were waited for; matrix products, arithmetic and copies ran while one was open for 12% of the time, Pallas kernels for 0%

commit v1 on v0

v1 whole, which is shorter than its diff:
```python
import functools

import jax
import jax.numpy as jnp
from jax import lax
from jax.experimental import pallas as pl
from jax.experimental.pallas import tpu as pltpu
from jax.sharding import PartitionSpec as P

EPSILON = 1e-06
LOG2E = 1.4426950408889634
NONE = -1e30
NX, NZ, NC, NB = 4, 4, 2, 4
HD = 128
HEADS = 3
SHARD = 128
FRAME = 256
OWN = 512
KEYS = 4096
F32 = jnp.float32
BF16 = jnp.bfloat16
VMEM_LIMIT = 56 * 1024 * 1024


def params():
    return pltpu.CompilerParams(vmem_limit_bytes=VMEM_LIMIT)


def split_bf16(value, count):
    parts = []
    for _ in range(count):
        part = value.astype(BF16).astype(F32)
        parts.append(part)
        value = value - part
    return parts


def tm_index(x, z, c):
    return (x * NZ + z) * NC + c


def shift_tm(block, dx=0, dz=0, swap=False):
    route = []
    for x in range(NX):
        for z in range(NZ):
            for c in range(NC):
                target = tm_index((x + dx) % NX, (z + dz) % NZ, 1 - c if swap else c)
                route.append((tm_index(x, z, c), target))
    return lax.ppermute(block, "tm", route)


def shift_band(block, db):
    return lax.ppermute(block, "band", [(i, (i + db) % NB) for i in range(NB)])


def halo(block, dt, db):
    count = lax.axis_size("tm")
    route = []
    for t in range(count):
        for b in range(NB):
            if t + dt < count and 0 <= b + db < NB:
                route.append((t * NB + b, (t + dt) * NB + b + db))
    return lax.ppermute(block, ("tm", "band"), route)


def fold_kernel(embed_ref, bias_ref, shift_ref, scale_ref, qkv_ref, out_ref, rows_ref, left, total):
    step = pl.program_id(0)
    width = left.shape[1]
    chunk = qkv_ref.shape[1]

    @pl.when(step == 0)
    def _():
        gain = 1.0 + scale_ref[...]
        for lo in range(0, 512, 64):
            weight = embed_ref[lo : lo + 64, :].astype(F32)
            centred = weight - jnp.mean(weight, axis=-1, keepdims=True)
            left[lo : lo + 64, :] = (centred * gain).astype(BF16)
        bias = bias_ref[...]
        bias = (bias - jnp.mean(bias, axis=-1, keepdims=True)) * gain
        extra = jnp.zeros((16, width), F32)
        place = lax.broadcasted_iota(jnp.int32, (16, width), 0)
        for at, part in enumerate(split_bf16(bias, 3) + split_bf16(shift_ref[...], 3)):
            extra = jnp.where(place == at, part, extra)
        left[512:528, :] = extra.astype(BF16)

    columns = pl.ds(pl.multiple_of(step * chunk, chunk), chunk)
    right = jnp.concatenate([qkv_ref[i] for i in range(9)], axis=1)
    part = jnp.dot(left[:, columns], right, preferred_element_type=F32)

    @pl.when(step == 0)
    def _():
        total[...] = part

    @pl.when(step > 0)
    def _():
        total[...] += part

    @pl.when(step == pl.num_programs(0) - 1)
    def _():
        out_ref[...] = total[0:512, :].astype(BF16)
        rows = total[512:528, :]
        place = lax.broadcasted_iota(jnp.int32, (8, 1152), 0)
        bias = rows[0:1] + rows[1:2] + rows[2:3]
        moved = rows[3:4] + rows[4:5] + rows[5:6]
        rows_ref[...] = jnp.where(place == 0, bias, jnp.where(place == 1, moved, 0.0))


def fold(embed_weight, embed_bias, mod_shift, mod_scale, qkv):
    chunk = 512
    steps = qkv.shape[1] // chunk
    row = pl.BlockSpec((1, 3072), lambda k: (0, 0))
    return pl.pallas_call(
        fold_kernel,
        grid=(steps,),
        in_specs=[
            pl.BlockSpec((512, 3072), lambda k: (0, 0)),
            row,
            row,
            row,
            pl.BlockSpec((9, chunk, HD), lambda k: (0, k, 0)),
        ],
        out_specs=[
            pl.BlockSpec((512, 1152), lambda k: (0, 0)),
            pl.BlockSpec((8, 1152), lambda k: (0, 0)),
        ],
        out_shape=[
            jax.ShapeDtypeStruct((512, 1152), BF16),
            jax.ShapeDtypeStruct((8, 1152), F32),
        ],
        scratch_shapes=[pltpu.VMEM((528, 3072), BF16), pltpu.VMEM((528, 1152), F32)],
        compiler_params=params(),
        cost_estimate=pl.CostEstimate(
            flops=2 * 528 * 3072 * 1152, bytes_accessed=12000000, transcendentals=0
        ),
    )(embed_weight, embed_bias[None], mod_shift[None], mod_scale[None], qkv)


def conv_kernel(
    slots_ref,
    cur_ref,
    prev_ref,
    up_cur_ref,
    down_cur_ref,
    up_prev_ref,
    down_prev_ref,
    gain_ref,
    bias_ref,
    embed_ref,
    embed_bias_ref,
    weight_ref,
    out_ref,
    send_ref,
    act,
    total,
):
    step = pl.program_id(0)

    @pl.when(step == 0)
    def _():
        total[...] = jnp.zeros_like(total)
        place = lax.broadcasted_iota(jnp.int32, (80, 512), 0) % 8
        for slot in range(4):
            up, mid, down = (
                (up_prev_ref, prev_ref, down_prev_ref)
                if slot < 2
                else (up_cur_ref, cur_ref, down_cur_ref)
            )
            at = slot % 2
            cells = jnp.concatenate(
                [
                    up[at, 0].astype(F32),
                    mid[at].astype(F32).reshape(64, 512),
                    down[at, 0].astype(F32),
                ],
                axis=0,
            )
            mean_square = jnp.mean(cells * cells, axis=-1, keepdims=True)
            scaled = cells * lax.rsqrt(mean_square + EPSILON) * gain_ref[...]
            active = (scaled * jax.nn.sigmoid(scaled)).astype(BF16).astype(F32)
            act[0, slot] = jnp.where(place == 0, 0.0, pltpu.roll(active, 1, 0))
            act[1, slot] = active
            act[2, slot] = jnp.where(place == 7, 0.0, pltpu.roll(active, 79, 0))

    tap_time = step // 3
    rows = pl.ds(pl.multiple_of((step % 3) * 8, 8), 64)
    part = total[...]
    for tap_col in range(3):
        piece = jnp.concatenate(
            [act[tap_col, slots_ref[i * 3 + tap_time], rows, :] for i in range(2)], axis=0
        ).astype(BF16)
        part = part + jnp.dot(piece, weight_ref[0, 0, tap_col], preferred_element_type=F32)
    total[...] = part

    @pl.when(step == pl.num_programs(0) - 1)
    def _():
        inputs = cur_ref[...].astype(F32).reshape(SHARD, 512)
        section = (inputs + bias_ref[...] + total[...]).astype(BF16)
        out_ref[...] = section.reshape(out_ref.shape)
        send_ref[0:SHARD, :] = section
        embedded = (
            jnp.dot(section, embed_ref[...], preferred_element_type=F32) + embed_bias_ref[...]
        )
        center = embedded - jnp.mean(embedded, axis=-1, keepdims=True)
        spread = jnp.mean(center * center, axis=-1, keepdims=True)
        scale = lax.rsqrt(spread + EPSILON)
        across = jnp.transpose(jnp.broadcast_to(scale, (SHARD, SHARD)))[0:16]
        high, low = split_bf16(across, 2)
        tail = jnp.concatenate([high, low, jnp.zeros((16, 256), F32)], axis=1)
        place = lax.broadcasted_iota(jnp.int32, (16, 512), 0)
        send_ref[SHARD : SHARD + 16, :] = jnp.where(place == 0, tail, 0.0).astype(BF16)


def conv(slots, pieces, norm_gain, conv_bias, embed_weight, embed_bias, conv_weight):
    def whole(shape):
        return pl.BlockSpec(shape, lambda k, s: (0,) * len(shape))

    return pl.pallas_call(
        conv_kernel,
        grid_spec=pltpu.PrefetchScalarGridSpec(
            num_scalar_prefetch=1,
            grid=(9,),
            in_specs=[whole(piece.shape) for piece in pieces]
            + [
                whole((1, 512)),
                whole((1, 512)),
                whole((512, 3072)),
                whole((1, 3072)),
                pl.BlockSpec((1, 1, 3, 512, 512), lambda k, s: (k // 3, k % 3, 0, 0, 0)),
            ],
            out_specs=[whole((2, 8, 8, 512)), whole((SHARD + 16, 512))],
            scratch_shapes=[pltpu.VMEM((3, 4, 80, 512), F32), pltpu.VMEM((SHARD, 512), F32)],
        ),
        out_shape=[
            jax.ShapeDtypeStruct((2, 8, 8, 512), BF16),
            jax.ShapeDtypeStruct((SHARD + 16, 512), BF16),
        ],
        compiler_params=params(),
        cost_estimate=pl.CostEstimate(
            flops=2 * 128 * 13824 * 512, bytes_accessed=18000000, transcendentals=0
        ),
    )(slots, *pieces, norm_gain[None], conv_bias[None], embed_weight, embed_bias[None], conv_weight)


def normed(values, gain):
    mean_square = jnp.mean(values * values, axis=-1, keepdims=True)
    return (values * lax.rsqrt(mean_square + EPSILON) * gain).astype(BF16)


def query_kernel(band_ref, s0, s1, s3, s2, weight_ref, rows_ref, gain_ref, q_ref, xr_ref):
    band = band_ref[0]
    place = lax.broadcasted_iota(jnp.int32, (16, 512), 0)
    tail = jnp.zeros((16, 512), F32)
    for back, ref in ((0, s0), (1, s1), (3, s3), (2, s2)):
        source = lax.rem(band + (NB - back), NB)
        cells = ref[0:SHARD, :]
        extra = ref[SHARD : SHARD + 16, :].astype(F32)
        tail = jnp.where(place == source, extra[0:1, :], tail)
        across = extra[0:1, 0:HD] + extra[0:1, HD : 2 * HD]
        scale = jnp.transpose(jnp.broadcast_to(across, (HD, HD)))
        projected = jnp.dot(cells, weight_ref[...], preferred_element_type=F32) + rows_ref[0:1, :]
        for head in range(HEADS):
            lanes = slice(head * HD, (head + 1) * HD)
            values = normed(projected[:, lanes] * scale + rows_ref[1:2, lanes], gain_ref[...])
            for i in range(2):
                rows = pl.ds(pl.multiple_of(i * FRAME + source * 64, 64), 64)
                q_ref[head, rows, :] = values[i * 64 : (i + 1) * 64]
        for i in range(2):
            rows = pl.ds(pl.multiple_of(i * FRAME + source * 64, 64), 64)
            xr_ref[rows, :] = cells[i * 64 : (i + 1) * 64]
    xr_ref[OWN : OWN + 16, :] = tail.astype(BF16)


def queries_of(band, shards, weight, rows, gain):
    smem = pl.BlockSpec(memory_space=pltpu.SMEM)
    vmem = pl.BlockSpec(memory_space=pltpu.VMEM)
    return pl.pallas_call(
        query_kernel,
        in_specs=[smem] + [vmem] * 7,
        out_specs=[vmem, vmem],
        out_shape=[
            jax.ShapeDtypeStruct((HEADS, OWN, HD), BF16),
            jax.ShapeDtypeStruct((OWN + 16, 512), BF16),
        ],
        compiler_params=params(),
        cost_estimate=pl.CostEstimate(
            flops=2 * 512 * 512 * 384, bytes_accessed=2000000, transcendentals=0
        ),
    )(band, *shards, weight, rows, gain[None])


def attend_kernel(
    info_ref, q0, q1, q3, q2, a0, a1, a3, a2, b0, b1, b3, b2, weight_ref, rows_ref, gain_ref,
    o0, o1, o3, o2, key_t, value_x, total, peak,
):
    x_here, core = info_ref[16], info_ref[17]
    value_x[:, :, HD : 2 * HD] = jnp.ones((HEADS, KEYS, HD), BF16)
    for swap, refs in ((0, (a0, a1, a3, a2)), (1, (b0, b1, b3, b2))):
        for back, ref in zip((0, 1, 3, 2), refs):
            source = lax.rem(x_here + (NX - back), NX)
            core_at = core if swap == 0 else 1 - core
            extra = ref[OWN : OWN + 16, :].astype(F32)
            across = extra[:, 0:HD] + extra[:, HD : 2 * HD]
            down = jnp.transpose(
                jnp.concatenate([across, jnp.zeros((HD - 16, HD), F32)], axis=0)
            )
            for i in range(2):
                scale = jnp.concatenate(
                    [down[i * 64 : (i + 1) * 64, b : b + 1] for b in range(NB)], axis=0
                )
                projected = (
                    jnp.dot(
                        ref[i * FRAME : (i + 1) * FRAME, :],
                        weight_ref[...],
                        preferred_element_type=F32,
                    )
                    + rows_ref[0:1, :]
                ) * scale + rows_ref[1:2, :]
                start = pl.multiple_of((source * 4 + core_at * 2 + i) * FRAME, FRAME)
                for head in range(HEADS):
                    keys = normed(projected[:, head * HD : (head + 1) * HD], gain_ref[...])
                    key_t[head, :, pl.ds(start, FRAME)] = jnp.transpose(keys)
                    value_x[head, pl.ds(start, FRAME), 0:HD] = projected[
                        :, (HEADS + head) * HD : (HEADS + head + 1) * HD
                    ].astype(BF16)

    factor = LOG2E / HD**0.5

    for group, (q_ref, o_ref) in enumerate(((q0, o0), (q1, o1), (q3, o3), (q2, o2))):

        def one_frame(i, carry, group=group, q_ref=q_ref, o_ref=o_ref):
            first = info_ref[group * 4 + i * 2]
            count = info_ref[group * 4 + i * 2 + 1]
            base = pl.multiple_of(i * FRAME, FRAME)
            total[...] = jnp.zeros_like(total)
            peak[...] = jnp.full_like(peak, NONE)

            def block(start, size):
                for head in range(HEADS):
                    scores = (
                        jnp.dot(
                            q_ref[head, pl.ds(base, FRAME), :],
                            key_t[head, :, pl.ds(start, size)],
                            preferred_element_type=F32,
                        )
                        * factor
                    )
                    old = peak[head][:, 0:1]
                    new = jnp.maximum(old, jnp.max(scores, axis=-1, keepdims=True))
                    weights = jnp.exp2(scores - new).astype(BF16)
                    mixed = jnp.dot(
                        weights,
                        value_x[head, pl.ds(start, size), :],
                        preferred_element_type=F32,
                    )
                    total[head] = total[head] * jnp.exp2(old - new) + mixed
                    peak[head] = jnp.broadcast_to(new, (FRAME, HD))

            def wide(j, c):
                block(pl.multiple_of((first + j * 4) * FRAME, FRAME), 4 * FRAME)
                return c

            def narrow(j, c):
                block(pl.multiple_of((first + j) * FRAME, FRAME), FRAME)
                return c

            wides = count // 4
            lax.fori_loop(0, wides, wide, 0)
            lax.fori_loop(wides * 4, count, narrow, 0)
            lane = lax.broadcasted_iota(jnp.int32, (FRAME, HD), 1)
            marks = jnp.zeros((FRAME, HD), F32)
            for head in range(HEADS):
                weight_sum = total[head, :, HD : 2 * HD]
                some = weight_sum > 0.0
                safe = jnp.where(some, weight_sum, 1.0)
                o_ref[pl.ds(pl.multiple_of(head * OWN + base, FRAME), FRAME), :] = (
                    total[head, :, 0:HD] / safe
                ).astype(BF16)
                level = jnp.where(some, peak[head] + jnp.log2(safe), NONE)
                for at, part in enumerate(split_bf16(level, 3)):
                    marks = jnp.where(lane == head * 3 + at, part, marks)
            for half in range(2):
                rows = pl.ds(
                    pl.multiple_of(HEADS * OWN + (i * 2 + half) * 16, 16), 16
                )
                o_ref[rows, :] = jnp.transpose(marks[half * HD : (half + 1) * HD])[0:16].astype(
                    BF16
                )
            return carry

        lax.fori_loop(0, 2, one_frame, 0)


def attend(info, queries, near, far, weight, rows, gain):
    smem = pl.BlockSpec(memory_space=pltpu.SMEM)
    vmem = pl.BlockSpec(memory_space=pltpu.VMEM)
    out = jax.ShapeDtypeStruct((HEADS * OWN + 64, HD), BF16)
    return pl.pallas_call(
        attend_kernel,
        in_specs=[smem] + [vmem] * 15,
        out_specs=[vmem] * 4,
        out_shape=[out] * 4,
        scratch_shapes=[
            pltpu.VMEM((HEADS, HD, KEYS), BF16),
            pltpu.VMEM((HEADS, KEYS, 2 * HD), BF16),
            pltpu.VMEM((HEADS, FRAME, 2 * HD), F32),
            pltpu.VMEM((HEADS, FRAME, HD), F32),
        ],
        compiler_params=params(),
        cost_estimate=pl.CostEstimate(
            flops=40000000000, bytes_accessed=10000000, transcendentals=0
        ),
    )(info, *queries, *near, *far, weight, rows, gain[None])


def merge_kernel(p0, p1, p2, p3, out_ref):
    for at in range(4):
        base = HEADS * OWN + at * 16
        columns = []
        for ref in (p0, p1, p2, p3):
            marks = ref[base : base + 16, :].astype(F32)
            columns.append(
                jnp.transpose(jnp.concatenate([marks, jnp.zeros((HD - 16, HD), F32)], axis=0))
            )
        for head in range(HEADS):
            rows = slice(head * OWN + at * HD, head * OWN + (at + 1) * HD)
            levels = [
                mark[:, head * 3 : head * 3 + 1]
                + mark[:, head * 3 + 1 : head * 3 + 2]
                + mark[:, head * 3 + 2 : head * 3 + 3]
                for mark in columns
            ]
            top = functools.reduce(jnp.maximum, levels)
            shares = [jnp.exp2(level - top) for level in levels]
            weight_sum = functools.reduce(jnp.add, shares)
            mixed = functools.reduce(
                jnp.add,
                [
                    ref[rows, :].astype(F32) * share
                    for ref, share in zip((p0, p1, p2, p3), shares)
                ],
            )
            out_ref[head, at * HD : (at + 1) * HD, :] = (mixed / weight_sum).astype(BF16)


def merge(parts):
    vmem = pl.BlockSpec(memory_space=pltpu.VMEM)
    return pl.pallas_call(
        merge_kernel,
        in_specs=[vmem] * 4,
        out_specs=vmem,
        out_shape=jax.ShapeDtypeStruct((HEADS, OWN, HD), BF16),
        compiler_params=params(),
    )(*parts)


def frame_bounds(frames, lengths):
    ends = jnp.cumsum(lengths)
    starts = ends - lengths
    inside = (frames[:, None] >= starts[None, :]) & (frames[:, None] < ends[None, :])
    first = jnp.sum(jnp.where(inside, starts[None, :], 0), axis=1)
    last = jnp.sum(jnp.where(inside, ends[None, :], 0), axis=1)
    return first, last


def per_device(
    section_in,
    norm_gain,
    conv_weight,
    conv_bias,
    lengths,
    embed_weight,
    embed_bias,
    mod_shift,
    mod_scale,
    qkv_weight,
    q_gain,
    k_gain,
):
    place = lax.axis_index("tm")
    band = lax.axis_index("band")
    x_here, z_here, core = place // (NZ * NC), place // NC % NZ, place % NC
    top, bottom = section_in[:, 0:1], section_in[:, 7:8]
    pieces = (
        section_in,
        halo(section_in, 1, 0),
        halo(bottom, 0, 1),
        halo(top, 0, -1),
        halo(bottom, 1, 1),
        halo(top, 1, -1),
    )
    qkv = jnp.transpose(qkv_weight, (1, 2, 0, 3)).reshape(9, 3072, HD)
    folded, rows = fold(embed_weight, embed_bias, mod_shift, mod_scale, qkv)

    own = place * 2 + jnp.arange(2, dtype=jnp.int32)
    own_first, _ = frame_bounds(own, lengths)
    taps = jnp.arange(3, dtype=jnp.int32)
    slots = jnp.maximum(own[:, None] - 2 + taps[None, :], own_first[:, None]) - (place * 2 - 2)
    section_out, send = conv(
        slots.reshape(-1).astype(jnp.int32),
        pieces,
        norm_gain,
        conv_bias,
        embed_weight,
        embed_bias,
        conv_weight,
    )
    shards = (send, shift_band(send, 1), shift_band(send, 3), shift_band(send, 2))
    query, xr = queries_of(
        band[None].astype(jnp.int32), shards, folded[:, 0:384], rows[:, 0:384], q_gain
    )
    queries = (query, shift_tm(query, dz=1), shift_tm(query, dz=3), shift_tm(query, dz=2))
    near = (xr, shift_tm(xr, dx=1), shift_tm(xr, dx=3), shift_tm(xr, dx=2))
    far = tuple(shift_tm(part, swap=True) for part in near)

    back = jnp.array([0, 1, 3, 2], jnp.int32)
    group_z = (z_here - back) % NZ
    query_frames = (
        x_here * 16 + group_z[:, None] * 4 + core * 2 + jnp.arange(2, dtype=jnp.int32)[None, :]
    ).reshape(-1)
    first, last = frame_bounds(query_frames, lengths)
    slot = jnp.arange(16, dtype=jnp.int32)
    key_frames = slot // 4 * 16 + z_here * 4 + slot % 4
    begin = jnp.sum((key_frames[None, :] < first[:, None]).astype(jnp.int32), axis=1)
    end = jnp.sum((key_frames[None, :] < last[:, None]).astype(jnp.int32), axis=1)
    info = jnp.concatenate(
        [
            jnp.stack([begin, end - begin], axis=1).reshape(-1),
            jnp.stack([x_here, core]),
        ]
    ).astype(jnp.int32)
    o0, o1, o3, o2 = attend(
        info, queries, near, far, folded[:, 384:1152], rows[:, 384:1152], k_gain
    )
    parts = (o0, shift_tm(o1, dz=3), shift_tm(o3, dz=1), shift_tm(o2, dz=2))
    attended = jnp.transpose(merge(parts), (1, 0, 2))
    return (section_out, attended)


def solution(mesh):
    return jax.shard_map(
        per_device,
        mesh=mesh,
        in_specs=(
            P("tm", "band", None, None),
            P(),
            P(),
            P(),
            P(),
            P(),
            P(),
            P(),
            P(),
            P(None, None, "band", None),
            P(),
            P(),
        ),
        out_specs=(P("tm", "band", None, None), P("tm", "band", None)),
        check_vma=False,
    )
```

time: 445 us -> 185 us (0.42)
  matrix products: 151 us -> 0 us
  Pallas kernels: 0 us -> 91.1 us
  local copies, waits for them, and re-layouts: 94.5 us -> 11.3 us
  waiting for transfers between devices: 111 us -> 47.9 us
  other arithmetic: 47.8 us -> 2.77 us
  starting transfers between devices: 6.98 us -> 30.4 us
  blocking collectives: 15.2 us -> 0 us
  between operations: 14.6 us -> 0.89 us
    dot_general x30 -> x0, matrix products: 151 us -> none  [the longest x8 79.8 us: running_block(): jnp.einsum('hqk,khd->qhd', weights.astype(jnp.bfloat16), pieces[1], prefe...]
    all_gather x2 -> x0, waiting for transfers between devices: 111 us -> none  [the longest x1 70.3 us: per_device(): lax.all_gather(key_rows, 'tm', axis=0, tiled=True)]
    pallas_call x0 -> x5, Pallas kernels: none -> 91.1 us  [the longest x1 58.5 us: attend(): pl.pallas_call(attend_kernel, in_specs=[smem] + [vmem] * 15, out_specs=[v...]
    unnamed x58 -> x38, local copies, waits for them, and re-layouts: 72.6 us -> 3.21 us
    ppermute x3 -> x21, waiting for transfers between devices: 0.01 us -> 47.9 us  [the longest x13 43.7 us: shift_tm(): return lax.ppermute(block, 'tm', route)]
    reduce_sum x21 -> x3, other arithmetic: 29.6 us -> 0.48 us  [the longest x2 0.27 us: frame_bounds(): first = jnp.sum(jnp.where(inside, starts[None, :], 0), axis=1)]
    ppermute x3 -> x21, starting transfers between devices: 6.68 us -> 30.4 us  [the longest x5 14.4 us: halo(): return lax.ppermute(block, ('tm', 'band'), route)]
    all_gather x1 -> x0, blocking collectives: 15.2 us -> none  [per_device(): piece = lax.all_gather(section_out, 'band', axis=1, tiled=True)]
  transfers between devices with their start and end apart: 5 -> 21, of which waited for: 2 -> 7; matrix products, arithmetic and copies ran while one was open for 12% -> 5% of each run, Pallas kernels for 0% -> 7%
where the time goes in v1:
time: 185 us; the launch traced here: 184 us
  Pallas kernels  91.1 us (49%)
  waiting for transfers between devices  47.9 us (26%)
  starting transfers between devices  30.4 us (16%)
  local copies, waits for them, and re-layouts  11.3 us (6%)
  other arithmetic  2.77 us (1%)
    pallas_call x1, Pallas kernels, attend(): pl.pallas_call(attend_kernel, in_specs=[smem] + [vmem] * 15, out_specs=[v...  58.5 us
    ppermute x13, waiting for transfers between devices, shift_tm(): return lax.ppermute(block, 'tm', route)  43.7 us
    ppermute x5, starting transfers between devices, halo(): return lax.ppermute(block, ('tm', 'band'), route)  14.4 us
    pallas_call x1, Pallas kernels, conv(): pl.pallas_call(conv_kernel, grid_spec=pltpu.PrefetchScalarGridSpec(num_sc...  13.2 us
    pallas_call x1, Pallas kernels, fold(): pl.pallas_call(fold_kernel, grid=(steps,), in_specs=[pl.BlockSpec((512, 3...  12.4 us
    ppermute x13, starting transfers between devices, shift_tm(): return lax.ppermute(block, 'tm', route)  11.8 us
    pallas_call x1, Pallas kernels, merge(): pl.pallas_call(merge_kernel, in_specs=[vmem] * 4, out_specs=vmem, out_sha...  4.44 us
    ppermute x3, starting transfers between devices, shift_band(): return lax.ppermute(block, 'band', [(i, (i + db) % NB) for i in range(NB)])  4.26 us
  transfers between devices with their start and end apart: 21, of which 7 were waited for; matrix products, arithmetic and copies ran while one was open for 5% of the time, Pallas kernels for 7%

profile of v1, /device:TPU:2, one launch (start us, length us, event | category | flops | bytes accessed | tf_op | source)
XLA Modules:
  0.0 184.4 jit_solution(1762259244611250428)
XLA Ops:
  0.6 0.7 fusion.8
  1.4 1.3 collective-permute-start.4
  2.7 1.3 collective-permute-start.2
  4.0 6.2 %collective-permute-start.3 = (bf16[2,1,8,512]{3,2,1,0:T(8,128)(2,1)S(1)}, bf16[2,1,8,512]{3,2,1,0:T(8,128)(2,1)S(1)}, u32[]{:S(2)}, u32[]{:S(2)}) collective-permute-start(bf16[2,1,8,512]{3,2,1,0:T(8,128)(2,1)S(1)} %get-tuple-element.27), channel_id=1, source_target_pairs={{0,5},{1,6},{2,7},{4,9},{5,10},{6,11},{8,13},{9,14},{10,15},{12,17... | collective-permute-start | bytes 49160 | tf_op jit(solution)/shard_map/ppermute | solution.py:63
  10.2 3.6 %collective-permute-start.1 = (bf16[2,1,8,512]{3,2,1,0:T(8,128)(2,1)S(1)}, bf16[2,1,8,512]{3,2,1,0:T(8,128)(2,1)S(1)}, u32[]{:S(2)}, u32[]{:S(2)}) collective-permute-start(bf16[2,1,8,512]{3,2,1,0:T(8,128)(2,1)S(1)} %get-tuple-element.27), channel_id=1, source_target_pairs={{0,1},{1,2},{2,3},{4,5},{5,6},{6,7},{8,9},{9,10},{10,11},{12,13},{... | collective-permute-start | bytes 49160 | tf_op jit(solution)/shard_map/ppermute | solution.py:63
  13.9 1.9 %collective-permute-start = (bf16[2,8,8,512]{3,2,1,0:T(8,128)(2,1)}, bf16[2,8,8,512]{3,2,1,0:T(8,128)(2,1)S(1)}, u32[]{:S(2)}, u32[]{:S(2)}) collective-permute-start(bf16[2,8,8,512]{3,2,1,0:T(8,128)(2,1)} %cur_ref.1), channel_id=1, source_target_pairs={{0,4},{1,5},{2,6},{3,7},{4,8},{5,9},{6,10},{7,11},{8,12},{9,13},{1... | collective-permute-start | bytes 393224 | tf_op jit(solution)/shard_map/ppermute | solution.py:63
  15.8 0.8 reduce-window.8
  18.3 4.2 %collective-permute-done.prev_ref = bf16[2,8,8,512]{3,2,1,0:T(8,128)(2,1)S(1)} collective-permute-done((bf16[2,8,8,512]{3,2,1,0:T(8,128)(2,1)}, bf16[2,8,8,512]{3,2,1,0:T(8,128)(2,1)S(1)}, u32[]{:S(2)}, u32[]{:S(2)}) %collective-permute-start) | collective-permute-done | bytes 131104 | tf_op jit(solution)/shard_map/ppermute | solution.py:63
  23.1 13.2 %shard_map.140 = (bf16[2,8,8,512]{3,2,1,0:T(8,128)(2,1)}, bf16[144,512]{1,0:T(8,128)(2,1)}) custom-call(s32[6]{0:T(128)} %sub.52.slots_ref, bf16[2,8,8,512]{3,2,1,0:T(8,128)(2,1)} %cur_ref.1, bf16[2,8,8,512]{3,2,1,0:T(8,128)(2,1)} %copy-done.6, bf16[2,1,8,512]{3,2,1,0:T(8,128)(2,1)} %copy-done.10, bf16[2,1,8,512]{3,2,1,0:T(8,128)(2,1)} %copy-done.8, ...), custom_call_target="tpu_custom_call" | custom-call | flops 1811939328 | bytes 18000000 | tf_op jit(solution)/shard_map/pallas_call | solution.py:217
  36.3 1.6 collective-permute-start.7
  37.9 2.6 %collective-permute-start.6 = (bf16[144,512]{1,0:T(8,128)(2,1)}, bf16[144,512]{1,0:T(8,128)(2,1)S(1)}, u32[]{:S(2)}, u32[]{:S(2)}) collective-permute-start(bf16[144,512]{1,0:T(8,128)(2,1)} %get-tuple-element.13.s0), channel_id=1, source_target_pairs={{0,3},{1,0},{2,1},{3,2},{4,7},{5,4},{6,5},{7,6},{8,11},{9,8},{10,9... | collective-permute-start | bytes 442376 | tf_op jit(solution)/shard_map/ppermute | solution.py:53
  40.6 12.4 %shard_map.141 = (bf16[512,1152]{1,0:T(8,128)(2,1)}, f32[8,1152]{1,0:T(8,128)}) custom-call(bf16[512,3072]{1,0:T(8,128)(2,1)} %embed_ref.3, f32[1,3072]{1,0:T(1,128)} %bitcast.23, f32[1,3072]{1,0:T(1,128)} %bitcast.31, f32[1,3072]{1,0:T(1,128)} %bitcast.32, bf16[9,3072,128]{2,1,0:T(8,128)(2,1)} %bitcast.30), custom_call_target="tpu_custom_call" | custom-call | flops 3737124864 | bytes 12000000 | tf_op jit(solution)/shard_map/pallas_call | solution.py:112
  53.0 1.3 slice.21.rows_ref
  54.3 1.8 slice.20.weight_ref
  56.8 2.6 %shard_map.142 = (bf16[3,512,128]{2,1,0:T(8,128)(2,1)}, bf16[528,512]{1,0:T(8,128)(2,1)}) custom-call(s32[1]{0:T(128)} %bitcast.9.band_ref, bf16[144,512]{1,0:T(8,128)(2,1)} %get-tuple-element.13.s0, bf16[144,512]{1,0:T(8,128)(2,1)} %copy-done.5, bf16[144,512]{1,0:T(8,128)(2,1)} %copy-done.4, bf16[144,512]{1,0:T(8,128)(2,1)} %copy-done.3, ...), custom_call_target="tpu_custom_call" | custom-call | flops 201326592 | bytes 2000000 | tf_op jit(solution)/shard_map/pallas_call | solution.py:276
  59.5 2.1 %collective-permute-start.13 = (bf16[528,512]{1,0:T(8,128)(2,1)}, bf16[528,512]{1,0:T(8,128)(2,1)S(1)}, u32[]{:S(2)}, u32[]{:S(2)}) collective-permute-start(bf16[528,512]{1,0:T(8,128)(2,1)} %get-tuple-element.17.a0), channel_id=1, source_target_pairs={{0,64},{4,68},{8,72},{12,76},{16,80},{20,84},{24,88},{28,92},{32,9... | collective-permute-start | bytes 1622024 | tf_op jit(solution)/shard_map/ppermute | solution.py:49
  61.6 1.4 collective-permute-start.12
  63.6 1.6 collective-permute-start.10
  65.2 1.0 collective-permute-start.9
  66.2 1.3 slice.23.rows_ref
  67.6 2.1 %slice.22.weight_ref = bf16[512,768]{1,0:T(8,128)(2,1)} slice(bf16[512,1152]{1,0:T(8,128)(2,1)} %get-tuple-element.14), slice={[0:512], [384:1152]} | slice | bytes 1572864 | tf_op jit(solution)/shard_map/slice | solution.py:532
  69.8 3.4 %collective-permute-done.10.q2 = bf16[3,512,128]{2,1,0:T(8,128)(2,1)S(1)} collective-permute-done((bf16[3,512,128]{2,1,0:T(8,128)(2,1)}, bf16[3,512,128]{2,1,0:T(8,128)(2,1)S(1)}, u32[]{:S(2)}, u32[]{:S(2)}) %collective-permute-start.10) | collective-permute-done | bytes 393248 | tf_op jit(solution)/shard_map/ppermute | solution.py:49
  73.2 3.2 %collective-permute-done.13.a2 = bf16[528,512]{1,0:T(8,128)(2,1)S(1)} collective-permute-done((bf16[528,512]{1,0:T(8,128)(2,1)}, bf16[528,512]{1,0:T(8,128)(2,1)S(1)}, u32[]{:S(2)}, u32[]{:S(2)}) %collective-permute-start.13) | collective-permute-done | bytes 540704 | tf_op jit(solution)/shard_map/ppermute | solution.py:49
  76.4 7.8 %collective-permute-done.12.a3 = bf16[528,512]{1,0:T(8,128)(2,1)S(1)} collective-permute-done((bf16[528,512]{1,0:T(8,128)(2,1)}, bf16[528,512]{1,0:T(8,128)(2,1)S(1)}, u32[]{:S(2)}, u32[]{:S(2)}) %collective-permute-start.12) | collective-permute-done | bytes 540704 | tf_op jit(solution)/shard_map/ppermute | solution.py:49
  84.9 1.9 %collective-permute-start.8 = (bf16[3,512,128]{2,1,0:T(8,128)(2,1)}, bf16[3,512,128]{2,1,0:T(8,128)(2,1)}, u32[]{:S(2)}, u32[]{:S(2)}) collective-permute-start(bf16[3,512,128]{2,1,0:T(8,128)(2,1)} %get-tuple-element.16.q0), channel_id=1, source_target_pairs={{0,8},{4,12},{8,16},{12,20},{16,24},{20,28},{24,0},{28,4},{32,40},... | collective-permute-start | bytes 1179656 | tf_op jit(solution)/shard_map/ppermute | solution.py:49
  87.6 10.2 %collective-permute-done.8.q1 = bf16[3,512,128]{2,1,0:T(8,128)(2,1)} collective-permute-done((bf16[3,512,128]{2,1,0:T(8,128)(2,1)}, bf16[3,512,128]{2,1,0:T(8,128)(2,1)}, u32[]{:S(2)}, u32[]{:S(2)}) %collective-permute-start.8) | collective-permute-done | bytes 393248 | tf_op jit(solution)/shard_map/ppermute | solution.py:49
  98.8 58.5 %shard_map.143 = (bf16[1600,128]{1,0:T(8,128)(2,1)}, bf16[1600,128]{1,0:T(8,128)(2,1)}, bf16[1600,128]{1,0:T(8,128)(2,1)}, bf16[1600,128]{1,0:T(8,128)(2,1)}) custom-call(s32[18]{0:T(128)} %pad_add_fusion.1.info_ref, bf16[3,512,128]{2,1,0:T(8,128)(2,1)} %get-tuple-element.16.q0, bf16[3,512,128]{2,1,0:T(8,128)(2,1)} %collective-permute-done.8.q1, ...), custom_call_target="tpu_custom_call" | custom-call | flops 40000000000 | bytes 10000000 | tf_op jit(solution)/shard_map/pallas_call | solution.py:397
  158.0 1.3 collective-permute-start.19
  160.1 9.9 %collective-permute-done.18.p1 = bf16[1600,128]{1,0:T(8,128)(2,1)S(1)} collective-permute-done((bf16[1600,128]{1,0:T(8,128)(2,1)}, bf16[1600,128]{1,0:T(8,128)(2,1)S(1)}, u32[]{:S(2)}, u32[]{:S(2)}) %collective-permute-start.18) | collective-permute-done | bytes 409632 | tf_op jit(solution)/shard_map/ppermute | solution.py:49
  169.9 9.1 %collective-permute-done.19.p2 = bf16[1600,128]{1,0:T(8,128)(2,1)S(1)} collective-permute-done((bf16[1600,128]{1,0:T(8,128)(2,1)}, bf16[1600,128]{1,0:T(8,128)(2,1)S(1)}, u32[]{:S(2)}, u32[]{:S(2)}) %collective-permute-start.19) | collective-permute-done | bytes 409632 | tf_op jit(solution)/shard_map/ppermute | solution.py:49
  179.1 0.7 copy-done.1
  180.0 4.4 %shard_map.144 = bf16[3,512,128]{2,1,0:T(8,128)(2,1)} custom-call(bf16[1600,128]{1,0:T(8,128)(2,1)} %get-tuple-element.18.p0, bf16[1600,128]{1,0:T(8,128)(2,1)} %copy-done, bf16[1600,128]{1,0:T(8,128)(2,1)} %copy-done.1, bf16[1600,128]{1,0:T(8,128)(2,1)} %copy-done.2), custom_call_target="tpu_custom_call" | custom-call | tf_op jit(solution)/shard_map/pallas_call | solution.py:447
  (75 shorter events, 7.9 us)
Async XLA Ops:
  1.4 16.8 %collective-permute-start.4 = (bf16[2,1,8,512]{3,2,1,0:T(8,128)(2,1)S(1)}, bf16[2,1,8,512]{3,2,1,0:T(8,128)(2,1)S(1)}, u32[]{:S(2)}, u32[]{:S(2)}) collective-permute-start(bf16[2,1,8,512]{3,2,1,0:T(8,128)(2,1)S(1)} %get-tuple-element.26), channel_id=1, source_target_pairs={{1,4},{2,5},{3,6},{5,8},{6,9},{7,10},{9,12},{10,13},{11,14},{13,16... | collective-permute-start | bytes 49160 | tf_op jit(solution)/shard_map/ppermute | solution.py:63
  2.7 15.5 %collective-permute-start.2 = (bf16[2,1,8,512]{3,2,1,0:T(8,128)(2,1)S(1)}, bf16[2,1,8,512]{3,2,1,0:T(8,128)(2,1)S(1)}, u32[]{:S(2)}, u32[]{:S(2)}) collective-permute-start(bf16[2,1,8,512]{3,2,1,0:T(8,128)(2,1)S(1)} %get-tuple-element.26), channel_id=1, source_target_pairs={{1,0},{2,1},{3,2},{5,4},{6,5},{7,6},{9,8},{10,9},{11,10},{13,12},{... | collective-permute-start | bytes 49160 | tf_op jit(solution)/shard_map/ppermute | solution.py:63
  4.0 14.3 %collective-permute-start.3 = (bf16[2,1,8,512]{3,2,1,0:T(8,128)(2,1)S(1)}, bf16[2,1,8,512]{3,2,1,0:T(8,128)(2,1)S(1)}, u32[]{:S(2)}, u32[]{:S(2)}) collective-permute-start(bf16[2,1,8,512]{3,2,1,0:T(8,128)(2,1)S(1)} %get-tuple-element.27), channel_id=1, source_target_pairs={{0,5},{1,6},{2,7},{4,9},{5,10},{6,11},{8,13},{9,14},{10,15},{12,17... | collective-permute-start | bytes 49160 | tf_op jit(solution)/shard_map/ppermute | solution.py:63
  10.2 8.0 %collective-permute-start.1 = (bf16[2,1,8,512]{3,2,1,0:T(8,128)(2,1)S(1)}, bf16[2,1,8,512]{3,2,1,0:T(8,128)(2,1)S(1)}, u32[]{:S(2)}, u32[]{:S(2)}) collective-permute-start(bf16[2,1,8,512]{3,2,1,0:T(8,128)(2,1)S(1)} %get-tuple-element.27), channel_id=1, source_target_pairs={{0,1},{1,2},{2,3},{4,5},{5,6},{6,7},{8,9},{9,10},{10,11},{12,13},{... | collective-permute-start | bytes 49160 | tf_op jit(solution)/shard_map/ppermute | solution.py:63
  13.9 8.6 %collective-permute-start = (bf16[2,8,8,512]{3,2,1,0:T(8,128)(2,1)}, bf16[2,8,8,512]{3,2,1,0:T(8,128)(2,1)S(1)}, u32[]{:S(2)}, u32[]{:S(2)}) collective-permute-start(bf16[2,8,8,512]{3,2,1,0:T(8,128)(2,1)} %cur_ref.1), channel_id=1, source_target_pairs={{0,4},{1,5},{2,6},{3,7},{4,8},{5,9},{6,10},{7,11},{8,12},{9,13},{1... | collective-permute-start | bytes 393224 | tf_op jit(solution)/shard_map/ppermute | solution.py:63
  18.2 4.3 %copy-start.7 = (bf16[2,1,8,512]{3,2,1,0:T(8,128)(2,1)}, bf16[2,1,8,512]{3,2,1,0:T(8,128)(2,1)S(1)}, u32[]{:S(2)}) copy-start(bf16[2,1,8,512]{3,2,1,0:T(8,128)(2,1)S(1)} %collective-permute-done.4.down_prev_ref) | copy-start | bytes 49156
  18.2 4.3 %copy-start.8 = (bf16[2,1,8,512]{3,2,1,0:T(8,128)(2,1)}, bf16[2,1,8,512]{3,2,1,0:T(8,128)(2,1)S(1)}, u32[]{:S(2)}) copy-start(bf16[2,1,8,512]{3,2,1,0:T(8,128)(2,1)S(1)} %collective-permute-done.2.down_cur_ref) | copy-start | bytes 49156
  18.2 4.3 %copy-start.9 = (bf16[2,1,8,512]{3,2,1,0:T(8,128)(2,1)}, bf16[2,1,8,512]{3,2,1,0:T(8,128)(2,1)S(1)}, u32[]{:S(2)}) copy-start(bf16[2,1,8,512]{3,2,1,0:T(8,128)(2,1)S(1)} %collective-permute-done.3.up_prev_ref) | copy-start | bytes 49156
  18.2 4.2 %copy-start.10 = (bf16[2,1,8,512]{3,2,1,0:T(8,128)(2,1)}, bf16[2,1,8,512]{3,2,1,0:T(8,128)(2,1)S(1)}, u32[]{:S(2)}) copy-start(bf16[2,1,8,512]{3,2,1,0:T(8,128)(2,1)S(1)} %collective-permute-done.1.up_cur_ref) | copy-start | bytes 49156
  36.3 19.8 %collective-permute-start.7 = (bf16[144,512]{1,0:T(8,128)(2,1)}, bf16[144,512]{1,0:T(8,128)(2,1)S(1)}, u32[]{:S(2)}, u32[]{:S(2)}) collective-permute-start(bf16[144,512]{1,0:T(8,128)(2,1)} %get-tuple-element.13.s0), channel_id=1, source_target_pairs={{0,2},{1,3},{2,0},{3,1},{4,6},{5,7},{6,4},{7,5},{8,10},{9,11},{10,... | collective-permute-start | bytes 442376 | tf_op jit(solution)/shard_map/ppermute | solution.py:53
  37.9 18.1 %collective-permute-start.6 = (bf16[144,512]{1,0:T(8,128)(2,1)}, bf16[144,512]{1,0:T(8,128)(2,1)S(1)}, u32[]{:S(2)}, u32[]{:S(2)}) collective-permute-start(bf16[144,512]{1,0:T(8,128)(2,1)} %get-tuple-element.13.s0), channel_id=1, source_target_pairs={{0,3},{1,0},{2,1},{3,2},{4,7},{5,4},{6,5},{7,6},{8,11},{9,8},{10,9... | collective-permute-start | bytes 442376 | tf_op jit(solution)/shard_map/ppermute | solution.py:53
  40.6 15.5 %collective-permute-start.5 = (bf16[144,512]{1,0:T(8,128)(2,1)}, bf16[144,512]{1,0:T(8,128)(2,1)S(1)}, u32[]{:S(2)}, u32[]{:S(2)}) collective-permute-start(bf16[144,512]{1,0:T(8,128)(2,1)} %get-tuple-element.13.s0), channel_id=1, source_target_pairs={{0,1},{1,2},{2,3},{3,0},{4,5},{5,6},{6,7},{7,4},{8,9},{9,10},{10,1... | collective-permute-start | bytes 442376 | tf_op jit(solution)/shard_map/ppermute | solution.py:53
  40.6 23.0 %copy-start.11 = (s32[4]{0:T(128)S(1)}, s32[4]{0:T(128)}, u32[]{:S(2)}) copy-start(s32[4]{0:T(128)} %constant.100) | copy-start | bytes 52
  59.5 16.9 %collective-permute-start.13 = (bf16[528,512]{1,0:T(8,128)(2,1)}, bf16[528,512]{1,0:T(8,128)(2,1)S(1)}, u32[]{:S(2)}, u32[]{:S(2)}) collective-permute-start(bf16[528,512]{1,0:T(8,128)(2,1)} %get-tuple-element.17.a0), channel_id=1, source_target_pairs={{0,64},{4,68},{8,72},{12,76},{16,80},{20,84},{24,88},{28,92},{32,9... | collective-permute-start | bytes 1622024 | tf_op jit(solution)/shard_map/ppermute | solution.py:49
  61.6 22.6 %collective-permute-start.12 = (bf16[528,512]{1,0:T(8,128)(2,1)}, bf16[528,512]{1,0:T(8,128)(2,1)S(1)}, u32[]{:S(2)}, u32[]{:S(2)}) collective-permute-start(bf16[528,512]{1,0:T(8,128)(2,1)} %get-tuple-element.17.a0), channel_id=1, source_target_pairs={{0,96},{4,100},{8,104},{12,108},{16,112},{20,116},{24,120},{28,124... | collective-permute-start | bytes 1622024 | tf_op jit(solution)/shard_map/ppermute | solution.py:49
  63.0 21.2 %collective-permute-start.11 = (bf16[528,512]{1,0:T(8,128)(2,1)}, bf16[528,512]{1,0:T(8,128)(2,1)S(1)}, u32[]{:S(2)}, u32[]{:S(2)}) collective-permute-start(bf16[528,512]{1,0:T(8,128)(2,1)} %get-tuple-element.17.a0), channel_id=1, source_target_pairs={{0,32},{4,36},{8,40},{12,44},{16,48},{20,52},{24,56},{28,60},{32,6... | collective-permute-start | bytes 1622024 | tf_op jit(solution)/shard_map/ppermute | solution.py:49
  63.6 9.6 %collective-permute-start.10 = (bf16[3,512,128]{2,1,0:T(8,128)(2,1)}, bf16[3,512,128]{2,1,0:T(8,128)(2,1)S(1)}, u32[]{:S(2)}, u32[]{:S(2)}) collective-permute-start(bf16[3,512,128]{2,1,0:T(8,128)(2,1)} %get-tuple-element.16.q0), channel_id=1, source_target_pairs={{0,16},{4,20},{8,24},{12,28},{16,0},{20,4},{24,8},{28,12},{32,48},... | collective-permute-start | bytes 1179656 | tf_op jit(solution)/shard_map/ppermute | solution.py:49
  65.2 19.7 %collective-permute-start.9 = (bf16[3,512,128]{2,1,0:T(8,128)(2,1)}, bf16[3,512,128]{2,1,0:T(8,128)(2,1)S(1)}, u32[]{:S(2)}, u32[]{:S(2)}) collective-permute-start(bf16[3,512,128]{2,1,0:T(8,128)(2,1)} %get-tuple-element.16.q0), channel_id=1, source_target_pairs={{0,24},{4,28},{8,0},{12,4},{16,8},{20,12},{24,16},{28,20},{32,56},... | collective-permute-start | bytes 1179656 | tf_op jit(solution)/shard_map/ppermute | solution.py:49
  73.2 24.7 %copy-start.17 = (bf16[3,512,128]{2,1,0:T(8,128)(2,1)}, bf16[3,512,128]{2,1,0:T(8,128)(2,1)S(1)}, u32[]{:S(2)}) copy-start(bf16[3,512,128]{2,1,0:T(8,128)(2,1)S(1)} %collective-permute-done.10.q2) | copy-start | bytes 1179652
  73.2 24.7 %collective-permute-start.14 = (bf16[528,512]{1,0:T(8,128)(2,1)}, bf16[528,512]{1,0:T(8,128)(2,1)S(1)}, u32[]{:S(2)}, u32[]{:S(2)}) collective-permute-start(bf16[528,512]{1,0:T(8,128)(2,1)} %get-tuple-element.17.a0), channel_id=1, source_target_pairs={{0,4},{4,0},{8,12},{12,8},{16,20},{20,16},{24,28},{28,24},{32,36},... | collective-permute-start | bytes 1622024 | tf_op jit(solution)/shard_map/ppermute | solution.py:49
  76.4 21.5 %copy-start.12 = (bf16[528,512]{1,0:T(8,128)(2,1)}, bf16[528,512]{1,0:T(8,128)(2,1)S(1)}, u32[]{:S(2)}) copy-start(bf16[528,512]{1,0:T(8,128)(2,1)S(1)} %collective-permute-done.13.a2) | copy-start | bytes 1622020
  76.4 21.5 %collective-permute-start.17 = (bf16[528,512]{1,0:T(8,128)(2,1)S(1)}, bf16[528,512]{1,0:T(8,128)(2,1)S(1)}, u32[]{:S(2)}, u32[]{:S(2)}) collective-permute-start(bf16[528,512]{1,0:T(8,128)(2,1)S(1)} %collective-permute-done.13.a2), channel_id=1, source_target_pairs={{0,4},{4,0},{8,12},{12,8},{16,20},{20,16},{24,28},{28,24},{32,36},... | collective-permute-start | bytes 1622024 | tf_op jit(solution)/shard_map/ppermute | solution.py:49
  84.2 13.7 %copy-start.13 = (bf16[528,512]{1,0:T(8,128)(2,1)}, bf16[528,512]{1,0:T(8,128)(2,1)S(1)}, u32[]{:S(2)}) copy-start(bf16[528,512]{1,0:T(8,128)(2,1)S(1)} %collective-permute-done.12.a3) | copy-start | bytes 1622020
  84.2 13.7 %collective-permute-start.16 = (bf16[528,512]{1,0:T(8,128)(2,1)S(1)}, bf16[528,512]{1,0:T(8,128)(2,1)}, u32[]{:S(2)}, u32[]{:S(2)}) collective-permute-start(bf16[528,512]{1,0:T(8,128)(2,1)S(1)} %collective-permute-done.12.a3), channel_id=1, source_target_pairs={{0,4},{4,0},{8,12},{12,8},{16,20},{20,16},{24,28},{28,24},{32,36},... | collective-permute-start | bytes 1622024 | tf_op jit(solution)/shard_map/ppermute | solution.py:49
  84.3 13.7 %copy-start.14 = (bf16[528,512]{1,0:T(8,128)(2,1)}, bf16[528,512]{1,0:T(8,128)(2,1)S(1)}, u32[]{:S(2)}) copy-start(bf16[528,512]{1,0:T(8,128)(2,1)S(1)} %collective-permute-done.11.a1) | copy-start | bytes 1622020
  84.3 13.6 %collective-permute-start.15 = (bf16[528,512]{1,0:T(8,128)(2,1)S(1)}, bf16[528,512]{1,0:T(8,128)(2,1)}, u32[]{:S(2)}, u32[]{:S(2)}) collective-permute-start(bf16[528,512]{1,0:T(8,128)(2,1)S(1)} %collective-permute-done.11.a1), channel_id=1, source_target_pairs={{0,4},{4,0},{8,12},{12,8},{16,20},{20,16},{24,28},{28,24},{32,36},... | collective-permute-start | bytes 1622024 | tf_op jit(solution)/shard_map/ppermute | solution.py:49
  84.9 13.0 %copy-start.18 = (bf16[3,512,128]{2,1,0:T(8,128)(2,1)}, bf16[3,512,128]{2,1,0:T(8,128)(2,1)S(1)}, u32[]{:S(2)}) copy-start(bf16[3,512,128]{2,1,0:T(8,128)(2,1)S(1)} %collective-permute-done.9.q3) | copy-start | bytes 1179652
  84.9 12.9 %collective-permute-start.8 = (bf16[3,512,128]{2,1,0:T(8,128)(2,1)}, bf16[3,512,128]{2,1,0:T(8,128)(2,1)}, u32[]{:S(2)}, u32[]{:S(2)}) collective-permute-start(bf16[3,512,128]{2,1,0:T(8,128)(2,1)} %get-tuple-element.16.q0), channel_id=1, source_target_pairs={{0,8},{4,12},{8,16},{12,20},{16,24},{20,28},{24,0},{28,4},{32,40},... | collective-permute-start | bytes 1179656 | tf_op jit(solution)/shard_map/ppermute | solution.py:49
  157.3 12.6 %collective-permute-start.18 = (bf16[1600,128]{1,0:T(8,128)(2,1)}, bf16[1600,128]{1,0:T(8,128)(2,1)S(1)}, u32[]{:S(2)}, u32[]{:S(2)}) collective-permute-start(bf16[1600,128]{1,0:T(8,128)(2,1)} %get-tuple-element.19), channel_id=1, source_target_pairs={{0,24},{4,28},{8,0},{12,4},{16,8},{20,12},{24,16},{28,20},{32,56},... | collective-permute-start | bytes 1228808 | tf_op jit(solution)/shard_map/ppermute | solution.py:49
  158.0 21.0 %collective-permute-start.19 = (bf16[1600,128]{1,0:T(8,128)(2,1)}, bf16[1600,128]{1,0:T(8,128)(2,1)S(1)}, u32[]{:S(2)}, u32[]{:S(2)}) collective-permute-start(bf16[1600,128]{1,0:T(8,128)(2,1)} %get-tuple-element.20), channel_id=1, source_target_pairs={{0,8},{4,12},{8,16},{12,20},{16,24},{20,28},{24,0},{28,4},{32,40},... | collective-permute-start | bytes 1228808 | tf_op jit(solution)/shard_map/ppermute | solution.py:49
  159.4 19.7 %collective-permute-start.20 = (bf16[1600,128]{1,0:T(8,128)(2,1)}, bf16[1600,128]{1,0:T(8,128)(2,1)S(1)}, u32[]{:S(2)}, u32[]{:S(2)}) collective-permute-start(bf16[1600,128]{1,0:T(8,128)(2,1)} %get-tuple-element.21), channel_id=1, source_target_pairs={{0,16},{4,20},{8,24},{12,28},{16,0},{20,4},{24,8},{28,12},{32,48},... | collective-permute-start | bytes 1228808 | tf_op jit(solution)/shard_map/ppermute | solution.py:49
  169.9 9.1 %copy-start = (bf16[1600,128]{1,0:T(8,128)(2,1)}, bf16[1600,128]{1,0:T(8,128)(2,1)S(1)}, u32[]{:S(2)}) copy-start(bf16[1600,128]{1,0:T(8,128)(2,1)S(1)} %collective-permute-done.18.p1) | copy-start | bytes 1228804
  (8 other events, 6.2 us)
